TPU v7x, 32 devices: a whole 2x2x4 slice. The times are simulated.
32 devices in a mesh: row: 2 (over core), col: 4 (over z), layer: 4 (over y, x).
Axes of the slice: x: 2, y: 2, z: 4, core: 2. Of those that a mesh axis runs over, the one named last changes fastest.
Arguments:
- panel_top: float32 [4, 1024, 1024], P('layer', 'row', 'col'), as said below
- panel_win: float32 [4, 1024, 1024], P('layer', 'col', 'row'), may hold values from -0.75 to 0.75
- panel_rest: float32 [4, 2688, 1024], P('layer', 'row', 'col'), may hold values from -0.75 to 0.75
- trail_rest: float32 [4, 2688, 1024], P('layer', 'row', 'col'), may hold values from -4 to 4
Outputs:
- factor_top: float32 [1024, 1024], P('row', 'col')
- factor_win: float32 [1024, 1024], P('col', 'row')
- factor_rest: float32 [2688, 1024], P(('row', 'layer'), 'col')
- schur: float32 [2688, 1024], P(('row', 'layer'), 'col')
Inputs may be any that keep to these rules, and one draw needn't show every extreme that they name: `panel_top`: each layer's block is symmetric, and the sum over the layers is positive definite with no eigenvalue under 0.25.
All inputs are finite; a program needn't handle non-finite values.
Results may differ from a plain program's by a relative error of at most 0.00021.
Values sent between devices are 32-bit elements; how exact they have to be, the bound alone decides.
A program may use at most 128 MiB of HBM per device.

v0:
```python
import jax
import jax.numpy as jnp
from jax import lax
from jax.sharding import PartitionSpec as P


def solve_right(factor, values):
    return jax.scipy.linalg.solve_triangular(factor, values.T, lower=True).T


def per_device(panel_top, panel_win, panel_rest, trail_rest):
    top_sum, win_sum = lax.psum((panel_top[0], panel_win[0]), "layer")
    rows_here, cols_here = top_sum.shape
    n_row = lax.axis_size("row")
    top_rows = lax.all_gather(top_sum, "row", axis=0, tiled=True)
    top_full = lax.all_gather(top_rows, "col", axis=1, tiled=True)
    factor_top = jnp.linalg.cholesky(top_full)
    window = lax.all_gather(win_sum, "row", axis=1, tiled=True)
    factor_win = solve_right(factor_top, window)
    rest_part = lax.psum_scatter(panel_rest[0], "layer", scatter_dimension=0, tiled=True)
    rest_full = lax.all_gather(rest_part, "col", axis=1, tiled=True)
    factor_rest = solve_right(factor_top, rest_full)
    panel_cols = factor_top.shape[1]
    shares = lax.all_to_all(factor_rest, "layer", split_axis=1, concat_axis=0, tiled=True)
    share_cols = panel_cols // lax.axis_size("layer")
    win_share = lax.dynamic_slice_in_dim(
        factor_win, lax.axis_index("layer") * share_cols, share_cols, 1
    )
    partial_trail = trail_rest[0]
    schur = lax.psum_scatter(
        partial_trail
        - jnp.dot(
            shares, win_share.T, precision=lax.Precision.HIGHEST, preferred_element_type=jnp.float32
        ),
        "layer",
        scatter_dimension=0,
        tiled=True,
    )
    top_block = lax.dynamic_slice(
        factor_top,
        (lax.axis_index("row") * rows_here, lax.axis_index("col") * cols_here),
        (rows_here, cols_here),
    )
    row_cols = panel_cols // n_row
    win_block = lax.dynamic_slice_in_dim(factor_win, lax.axis_index("row") * row_cols, row_cols, 1)
    rest_block = lax.dynamic_slice_in_dim(
        factor_rest, lax.axis_index("col") * cols_here, cols_here, 1
    )
    return (top_block, win_block, rest_block, schur)


def solution(mesh):
    return jax.shard_map(
        per_device,
        mesh=mesh,
        in_specs=(
            P("layer", "row", "col"),
            P("layer", "col", "row"),
            P("layer", "row", "col"),
            P("layer", "row", "col"),
        ),
        out_specs=(
            P("row", "col"),
            P("col", "row"),
            P(("row", "layer"), "col"),
            P(("row", "layer"), "col"),
        ),
        check_vma=False,
    )
```

profile of v0, /device:TPU:0, one launch (start us, length us, event | category | flops | bytes accessed | tf_op | source)
XLA Modules:
  0.0 609.8 jit_solution(14450535642443820278)
XLA Ops:
  7.2 2.0 copy.11
  9.3 57.8 %all-reduce.4.cloned.1.call-done = (f32[512,256]{0,1:T(8,128)}, f32[256,512]{1,0:T(8,128)}) async-done(((f32[512,256]{0,1:T(8,128)}, f32[256,512]{1,0:T(8,128)}), (f32[512,256]{0,1:T(8,128)}, f32[256,512]{1,0:T(8,128)})) %all-reduce.4.cloned.1.call-update) | async-done | bytes 1048592 | tf_op jit(solution)/shard_map/psum | solution.py:12
  67.9 9.8 %all-gather.5.cloned.1.call-done = f32[1024,256]{0,1:T(8,128)} async-done(((f32[512,256]{0,1:T(8,128)}), f32[1024,256]{0,1:T(8,128)}) %all-gather.5.cloned.1.call-update) | async-done | bytes 1048592 | tf_op jit(solution)/shard_map/all_gather | solution.py:15
  78.4 33.2 %reduce-scatter.3.cloned.1.call-done = f32[336,256]{1,0:T(8,128)} async-done(((f32[1344,256]{1,0:T(8,128)}), f32[336,256]{1,0:T(8,128)}) %reduce-scatter.3.cloned.1.call-update) | async-done | bytes 344080 | tf_op jit(solution)/shard_map/reduce_scatter | solution.py:20
  111.6 82.2 %all-gather.7.cloned.1.call-done = f32[1024,1024]{0,1:T(8,128)} async-done(((f32[1024,256]{0,1:T(8,128)}), f32[1024,1024]{0,1:T(8,128)}) %all-gather.7.cloned.1.call-update) | async-done | bytes 4194320 | tf_op jit(solution)/shard_map/all_gather | solution.py:16
  193.8 5.3 copy.12
  199.1 4.8 fusion
  204.0 1.9 copy-done
  205.9 11.7 %cholesky.223 = f32[128,128]{1,0:T(8,128)S(1)} custom-call(f32[128,128]{1,0:T(8,128)S(1)} %cholesky.580), custom_call_target="Cholesky" | custom-call | tf_op jit(solution)/shard_map/jit(cholesky)/cholesky | solution.py:17
  217.7 9.8 %custom-call.66 = f32[1,128,128]{1,2,0:T(8,128)S(1)} custom-call(f32[1,128,128]{2,1,0:T(8,128)S(1)} %get-tuple-element.105), custom_call_target="InvertDiagBlocksLowerTriangular" | custom-call | tf_op jit(solution)/shard_map/jit(cholesky)/cholesky | solution.py:17
  227.5 2.5 cholesky.255
  230.0 2.3 constant_dynamic-update-slice_fusion.53
  232.3 1.6 convolution_subtract_fusion.1
  233.9 12.0 %cholesky.244 = f32[128,128]{1,0:T(8,128)S(1)} custom-call(f32[128,128]{1,0:T(8,128)S(1)} %cholesky.584), custom_call_target="Cholesky" | custom-call | tf_op jit(solution)/shard_map/jit(cholesky)/cholesky | solution.py:17
  246.6 9.8 %custom-call.67 = f32[1,128,128]{1,2,0:T(8,128)S(1)} custom-call(f32[1,128,128]{2,1,0:T(8,128)S(1)} %get-tuple-element.102), custom_call_target="InvertDiagBlocksLowerTriangular" | custom-call | tf_op jit(solution)/shard_map/jit(cholesky)/cholesky | solution.py:17
  257.6 2.1 convolution_subtract_fusion.2
  259.8 11.7 %cholesky.468 = f32[128,128]{1,0:T(8,128)S(1)} custom-call(f32[128,128]{1,0:T(8,128)S(1)} %cholesky.589), custom_call_target="Cholesky" | custom-call | tf_op jit(solution)/shard_map/jit(cholesky)/cholesky | solution.py:17
  272.7 9.8 %custom-call.68 = f32[1,128,128]{1,2,0:T(8,128)S(1)} custom-call(f32[1,128,128]{2,1,0:T(8,128)S(1)} %get-tuple-element.99), custom_call_target="InvertDiagBlocksLowerTriangular" | custom-call | tf_op jit(solution)/shard_map/jit(cholesky)/cholesky | solution.py:17
  283.7 2.3 convolution_subtract_fusion.3
  286.1 11.8 %cholesky.487 = f32[128,128]{1,0:T(8,128)S(1)} custom-call(f32[128,128]{1,0:T(8,128)S(1)} %cholesky.594), custom_call_target="Cholesky" | custom-call | tf_op jit(solution)/shard_map/jit(cholesky)/cholesky | solution.py:17
  299.2 9.8 %custom-call.69 = f32[1,128,128]{1,2,0:T(8,128)S(1)} custom-call(f32[1,128,128]{2,1,0:T(8,128)S(1)} %get-tuple-element.96), custom_call_target="InvertDiagBlocksLowerTriangular" | custom-call | tf_op jit(solution)/shard_map/jit(cholesky)/cholesky | solution.py:17
  310.1 2.3 convolution_subtract_fusion.4
  312.5 11.7 %cholesky.506 = f32[128,128]{1,0:T(8,128)S(1)} custom-call(f32[128,128]{1,0:T(8,128)S(1)} %cholesky.599), custom_call_target="Cholesky" | custom-call | tf_op jit(solution)/shard_map/jit(cholesky)/cholesky | solution.py:17
  325.5 10.0 %custom-call.70 = f32[1,128,128]{1,2,0:T(8,128)S(1)} custom-call(f32[1,128,128]{2,1,0:T(8,128)S(1)} %get-tuple-element.93), custom_call_target="InvertDiagBlocksLowerTriangular" | custom-call | tf_op jit(solution)/shard_map/jit(cholesky)/cholesky | solution.py:17
  336.5 2.3 convolution_subtract_fusion.5
  338.8 11.7 %cholesky.526 = f32[128,128]{1,0:T(8,128)S(1)} custom-call(f32[128,128]{1,0:T(8,128)S(1)} %cholesky.604), custom_call_target="Cholesky" | custom-call | tf_op jit(solution)/shard_map/jit(cholesky)/cholesky | solution.py:17
  351.8 9.8 %custom-call.71 = f32[1,128,128]{1,2,0:T(8,128)S(1)} custom-call(f32[1,128,128]{2,1,0:T(8,128)S(1)} %get-tuple-element.90), custom_call_target="InvertDiagBlocksLowerTriangular" | custom-call | tf_op jit(solution)/shard_map/jit(cholesky)/cholesky | solution.py:17
  362.6 2.0 convolution_subtract_fusion.19
  364.7 12.1 %cholesky.546 = f32[128,128]{1,0:T(8,128)S(1)} custom-call(f32[128,128]{1,0:T(8,128)S(1)} %cholesky.609), custom_call_target="Cholesky" | custom-call | tf_op jit(solution)/shard_map/jit(cholesky)/cholesky | solution.py:17
  378.1 9.8 %custom-call.72 = f32[1,128,128]{1,2,0:T(8,128)S(1)} custom-call(f32[1,128,128]{2,1,0:T(8,128)S(1)} %get-tuple-element.87), custom_call_target="InvertDiagBlocksLowerTriangular" | custom-call | tf_op jit(solution)/shard_map/jit(cholesky)/cholesky | solution.py:17
  388.7 1.8 convolution_subtract_fusion.21
  390.5 11.7 %cholesky.564 = f32[128,128]{1,0:T(8,128)S(1)} custom-call(f32[128,128]{1,0:T(8,128)S(1)} %convolution_subtract_fusion.21), custom_call_target="Cholesky" | custom-call | tf_op jit(solution)/shard_map/jit(cholesky)/cholesky | solution.py:17
  409.2 6.6 %fusion.1 = (f32[1024,1024]{1,0:T(8,128)}, f32[1024,1024]{1,0:T(8,128)}) fusion(f32[1024,1024]{1,0:T(8,128)} %get-tuple-element.85, pred[]{:T(512)S(6)} %cholesky.579), kind=kLoop, calls=%fused_computation.6 | loop fusion | flops 4194304 | bytes 12582913 | tf_op jit(solution)/shard_map/jit(_solve_triangular)/triangular_solve | solution.py:8
  415.8 23.2 %while.1 = (s32[]{:T(128)}, f32[1024,1024]{1,0:T(8,128)}, s32[8,2]{0,1:T(2,128)S(1)}, f32[8,128,128]{2,1,0:T(8,128)S(1)}, s32[]{:T(128)}) while((s32[]{:T(128)}, f32[1024,1024]{1,0:T(8,128)}, s32[8,2]{0,1:T(2,128)S(1)}, f32[8,128,128]{2,1,0:T(8,128)S(1)}, s32[]{:T(128)}) %tuple.86), condition=%wide.while_cond, body=%wide.while_body.sunk | while | flops 2 | bytes 131189 | solution.py:8
  416.4 2.3 bitcast_dynamic-update-slice_fusion.2
  419.3 2.3 bitcast_dynamic-update-slice_fusion.2
  422.3 2.3 bitcast_dynamic-update-slice_fusion.2
  425.2 2.3 bitcast_dynamic-update-slice_fusion.2
  428.1 2.3 bitcast_dynamic-update-slice_fusion.2
  431.0 2.3 bitcast_dynamic-update-slice_fusion.2
  433.9 2.3 bitcast_dynamic-update-slice_fusion.2
  436.8 2.2 bitcast_dynamic-update-slice_fusion.2
  439.0 78.8 %custom-call.73 = f32[8,128,128]{1,2,0:T(8,128)S(1)} custom-call(f32[8,128,128]{2,1,0:T(8,128)S(1)} %get-tuple-element.11), custom_call_target="InvertDiagBlocksLowerTriangular" | custom-call | tf_op jit(solution)/shard_map/jit(_solve_triangular)/triangular_solve | solution.py:8
  517.8 1.9 constant_dynamic-update-slice_fusion.17
  519.8 1.3 convolution_subtract_fusion.18
  522.2 1.6 convolution_subtract_fusion.16
  524.7 1.8 convolution_subtract_fusion.15
  527.6 2.0 convolution_subtract_fusion.14
  531.6 2.3 convolution_subtract_fusion.13
  533.9 1.3 constant_dynamic-update-slice_fusion.42
  536.8 1.4 convolution_subtract_fusion.8
  538.6 1.5 convolution_subtract_fusion.7
  540.4 1.7 convolution_subtract_fusion.6
  542.4 1.8 convolution_subtract_fusion.11
  544.6 2.0 convolution_subtract_fusion.10
  546.8 2.2 convolution_subtract_fusion.9
  549.3 1.5 copy.17
  550.8 3.7 all-to-all-start
  555.6 2.7 convolution_subtract_fusion.17
  559.3 3.0 convolution_subtract_fusion.20
  563.2 8.6 %all-to-all-done = f32[336,4,256]{2,0,1:T(8,128)S(1)} async-done(((f32[336,4,256]{2,0,1:T(8,128)}), f32[336,4,256]{2,0,1:T(8,128)S(1)}, u32[]{:S(2)}, u32[]{:S(2)}) %all-to-all-start) | async-done | bytes 1376288 | tf_op jit(solution)/shard_map/all_to_all | solution.py:24
  571.8 3.7 convolution_subtract_fusion
  577.7 1.9 dynamic_slice.10
  580.3 22.4 %reduce-scatter.5.cloned.1.call-done = f32[336,256]{1,0:T(8,128)} async-done(((f32[1344,256]{1,0:T(8,128)}), f32[336,256]{1,0:T(8,128)}) %reduce-scatter.5.cloned.1.call-update) | async-done | bytes 344080 | tf_op jit(solution)/shard_map/reduce_scatter | solution.py:30
  (86 shorter events, 36.2 us)
Async XLA Ops:
  7.2 59.9 %all-reduce.4.cloned.1.call-start = ((), (), s32[]{:S(2)}) async-start(), calls=%async_computation.9 | async-start | bytes 2097152 | tf_op jit(solution)/shard_map/psum | solution.py:12
  9.3 68.4 %all-gather.5.cloned.1.call-start = ((), (), s32[]{:S(2)}) async-start(), calls=%async_computation.3 | async-start | bytes 1572864 | tf_op jit(solution)/shard_map/all_gather | solution.py:15
  67.1 44.5 %reduce-scatter.3.cloned.1.call-start = ((), (), s32[]{:S(2)}) async-start(), calls=%async_computation.6 | async-start | bytes 1720320 | tf_op jit(solution)/shard_map/reduce_scatter | solution.py:20
  67.9 125.9 %all-gather.7.cloned.1.call-start = ((), (), s32[]{:S(2)}) async-start(), calls=%async_computation.4 | async-start | bytes 5242880 | tf_op jit(solution)/shard_map/all_gather | solution.py:16
  77.7 440.1 %all-gather.9.cloned.1.call-start = ((), (), s32[]{:S(2)}) async-start(), calls=%async_computation.5 | async-start | bytes 1572864 | tf_op jit(solution)/shard_map/all_gather | solution.py:18
  78.3 455.6 %all-gather.11.cloned.1.call-start = ((), (), s32[]{:S(2)}) async-start(), calls=%async_computation.7 | async-start | bytes 1720320 | tf_op jit(solution)/shard_map/all_gather | solution.py:21
  204.0 1.9 copy-start
  530.6 1.0 copy-start.2
  533.9 4.7 copy-start.1
  550.8 21.0 %all-to-all-start = ((f32[336,4,256]{2,0,1:T(8,128)}), f32[336,4,256]{2,0,1:T(8,128)S(1)}, u32[]{:S(2)}, u32[]{:S(2)}) async-start(f32[336,4,256]{2,0,1:T(8,128)} %bitcast.147), calls=%async_computation.1 | async-start | bytes 2752512 | tf_op jit(solution)/shard_map/all_to_all | solution.py:24
  554.5 48.2 %reduce-scatter.5.cloned.1.call-start = ((), (), s32[]{:S(2)}) async-start(), calls=%async_computation.8 | async-start | bytes 1720320 | tf_op jit(solution)/shard_map/reduce_scatter | solution.py:30
Sparse Core Ops, SparseCore 0:
  11.6 55.4 all-reduce.3
  68.6 9.0 all-gather.4
  80.6 30.8 reduce-scatter.2
  113.0 80.7 all-gather.6
  195.2 7.5 all-gather.8
  204.2 35.0 all-gather.10
  575.7 26.9 reduce-scatter.4
where the time goes:
time: 620 us; the launch traced here: 610 us
  other arithmetic  263 us (42%)
  waiting for transfers between devices  215 us (35%)
  matrix products  65.7 us (11%)
  local copies, waits for them, and re-layouts  42.1 us (7%)
  between operations  19.8 us (3%)
    another operation x30, other arithmetic, per_device(): factor_top = jnp.linalg.cholesky(top_full)  172 us
    another operation x3, other arithmetic, solve_right(): return jax.scipy.linalg.solve_triangular(factor, values.T, lower=True).T  85.4 us
    all_gather x1, waiting for transfers between devices, per_device(): top_full = lax.all_gather(top_rows, 'col', axis=1, tiled=True)  82.2 us
    psum x1, waiting for transfers between devices, per_device(): top_sum, win_sum = lax.psum((panel_top[0], panel_win[0]), 'layer')  57.8 us
    another operation x30, matrix products, solve_right(): return jax.scipy.linalg.solve_triangular(factor, values.T, lower=True).T  38.9 us
    reduce_scatter x1, waiting for transfers between devices, per_device(): lax.psum_scatter(panel_rest[0], 'layer', scatter_dimension=0, tiled=True)  33.2 us
    another operation x14, matrix products, per_device(): factor_top = jnp.linalg.cholesky(top_full)  23.1 us
    another operation x24, local copies, waits for them, and re-layouts  23 us
  transfers between devices with their start and end apart: 8, of which 6 were waited for; matrix products, arithmetic and copies ran while one was open for 57% of the time, Pallas kernels for 0%

commit v1 on v0

v1 whole, which is shorter than its diff:
```python
import jax
import jax.numpy as jnp
from jax import lax
from jax.experimental import pallas as pl
from jax.experimental.pallas import tpu as pltpu
from jax.sharding import PartitionSpec as P

B = 128
HI = lax.Precision.HIGHEST


def dot(a, b, ca=1, cb=0):
    return lax.dot_general(
        a, b, (((ca,), (cb,)), ((), ())), precision=HI, preferred_element_type=jnp.float32
    )


def factor_block(a):
    n = B // 8
    sub = lax.broadcasted_iota(jnp.int32, (8, B), 0)
    lane = lax.broadcasted_iota(jnp.int32, (8, B), 1)
    left = [a[8 * t : 8 * t + 8, :] for t in range(n)]
    right = [jnp.where(lane == sub + 8 * t, 1.0, 0.0).astype(jnp.float32) for t in range(n)]
    for b in range(n):
        cols = [
            {t: jnp.broadcast_to(left[t][:, 8 * b + j : 8 * b + j + 1], (8, B)) for t in range(b, n)}
            for j in range(8)
        ]
        diag = jnp.zeros((8, B), jnp.float32)
        for i in range(8):
            diag = jnp.where(sub == i, cols[i][b], diag)
            inv = 1.0 / cols[i][b][i : i + 1, :]
            pivots = [cols[l][b][i : i + 1, :] for l in range(8)]
            row_l, row_r = left[b][i : i + 1, :], right[b][i : i + 1, :]
            for t in range(b, n):
                if t == b and i == 7:
                    continue
                m = cols[i][t] * inv
                if t == b:
                    m = jnp.where(sub > i, m, 0.0)
                for l in range(i + 1, 8):
                    cols[l][t] = cols[l][t] - m * pivots[l]
                left[t] = left[t] - m * row_l
                right[t] = right[t] - m * row_r
        scale = lax.rsqrt(diag)
        left[b] = left[b] * scale
        right[b] = right[b] * scale
    return jnp.concatenate(left, 0), jnp.concatenate(right, 0)


def chol_kernel(n_col, g_ref, u_ref, inv_ref, a_ref):
    pieces, rows, cols = g_ref.shape
    size = a_ref.shape[0]
    for p in range(pieces):
        r, c = p // n_col, p % n_col
        a_ref[r * rows : (r + 1) * rows, c * cols : (c + 1) * cols] = g_ref[p]
    blocks = size // B

    def step(k, carry):
        here = pl.ds(pl.multiple_of(k * B, B), B)
        u_diag, inv = factor_block(a_ref[here, here])
        inv_ref[k] = inv
        row = dot(inv, a_ref[here, :])
        at_row = lax.broadcasted_iota(jnp.int32, (B, size), 0) + k * B
        at_col = lax.broadcasted_iota(jnp.int32, (B, size), 1)
        row = jnp.where(at_col >= at_row, row, 0.0)
        u_ref[here, :] = row
        upper = lax.broadcasted_iota(jnp.int32, (B, B), 1) >= lax.broadcasted_iota(
            jnp.int32, (B, B), 0
        )
        u_ref[here, here] = jnp.where(upper, u_diag, 0.0)

        def update(r, carry):
            there = pl.ds(pl.multiple_of(r * B, B), B)
            a_ref[there, :] = a_ref[there, :] - dot(u_ref[here, there], u_ref[here, :], 0, 0)
            return carry

        return lax.fori_loop(k + 1, blocks, update, carry)

    lax.fori_loop(0, blocks, step, 0)


def solve_kernel(win_ref, rest_ref, trail_ref, u_ref, inv_ref, fw_ref, fr_ref, s_ref):
    blocks = inv_ref.shape[0]
    fw_ref[...] = win_ref[...]
    fr_ref[...] = rest_ref[...]
    for j in range(blocks):
        here, after = slice(j * B, (j + 1) * B), slice((j + 1) * B, blocks * B)
        for x_ref in (fw_ref, fr_ref):
            x = dot(x_ref[:, here], inv_ref[j], 1, 1)
            x_ref[:, here] = x
            if j + 1 < blocks:
                x_ref[:, after] = x_ref[:, after] - dot(x, u_ref[here, after])
    s_ref[...] = trail_ref[...] - dot(fr_ref[...], fw_ref[...], 1, 1)


def vmem(n):
    return [pl.BlockSpec(memory_space=pltpu.VMEM)] * n


def per_device(panel_top, panel_win, panel_rest, trail_rest):
    rows_here, cols_here = panel_top.shape[1:]
    n_row, n_col = lax.axis_size("row"), lax.axis_size("col")
    size = rows_here * n_row
    top_part = lax.psum_scatter(panel_top[0], "layer", scatter_dimension=0, tiled=True)
    top_all = lax.all_gather(top_part, ("row", "layer", "col"), axis=0, tiled=False)
    top_all, panel_win, panel_rest, trail_rest = lax.optimization_barrier(
        (top_all, panel_win, panel_rest, trail_rest)
    )
    rest_part = lax.psum_scatter(panel_rest[0], "layer", scatter_dimension=0, tiled=True)
    rest_full = lax.all_gather(rest_part, "col", axis=1, tiled=True)
    win_sum = lax.psum(panel_win[0], "layer")
    window = lax.all_gather(win_sum, "row", axis=1, tiled=True)
    trail = lax.psum_scatter(trail_rest[0], "layer", scatter_dimension=0, tiled=True)

    params = pltpu.CompilerParams(vmem_limit_bytes=40 * 2**20)
    upper, inverses = pl.pallas_call(
        lambda *refs: chol_kernel(n_col, *refs),
        out_shape=(
            jax.ShapeDtypeStruct((size, size), jnp.float32),
            jax.ShapeDtypeStruct((size // B, B, B), jnp.float32),
        ),
        in_specs=vmem(1),
        out_specs=tuple(vmem(2)),
        scratch_shapes=[pltpu.VMEM((size, size), jnp.float32)],
        compiler_params=params,
        cost_estimate=pl.CostEstimate(
            flops=80 * size**3, bytes_accessed=12 * size**2, transcendentals=0
        ),
        name="factor",
    )(top_all)
    factor_win, factor_rest, schur = pl.pallas_call(
        solve_kernel,
        out_shape=(
            jax.ShapeDtypeStruct(window.shape, jnp.float32),
            jax.ShapeDtypeStruct(rest_full.shape, jnp.float32),
            jax.ShapeDtypeStruct(trail.shape, jnp.float32),
        ),
        in_specs=vmem(5),
        out_specs=tuple(vmem(3)),
        compiler_params=params,
        name="solve",
    )(window, rest_full, trail, upper, inverses)

    top_block = lax.dynamic_slice(
        upper,
        (lax.axis_index("col") * cols_here, lax.axis_index("row") * rows_here),
        (cols_here, rows_here),
    ).T
    row_cols = size // n_row
    win_block = lax.dynamic_slice_in_dim(factor_win, lax.axis_index("row") * row_cols, row_cols, 1)
    rest_block = lax.dynamic_slice_in_dim(
        factor_rest, lax.axis_index("col") * cols_here, cols_here, 1
    )
    return (top_block, win_block, rest_block, schur)


def solution(mesh):
    return jax.shard_map(
        per_device,
        mesh=mesh,
        in_specs=(
            P("layer", "row", "col"),
            P("layer", "col", "row"),
            P("layer", "row", "col"),
            P("layer", "row", "col"),
        ),
        out_specs=(
            P("row", "col"),
            P("col", "row"),
            P(("row", "layer"), "col"),
            P(("row", "layer"), "col"),
        ),
        check_vma=False,
    )
```

time: 620 us -> 293 us (0.47); the launches traced: 610 us -> 293 us
  other arithmetic: 263 us -> 0 us
  Pallas kernels: 0 us -> 69 us
  matrix products: 65.7 us -> 0 us
  local copies, waits for them, and re-layouts: 42.1 us -> 12.5 us
  waiting for transfers between devices: 215 us -> 197 us
    another operation x33 -> x0, other arithmetic: 258 us -> none  [the longest x30 172 us: per_device(): factor_top = jnp.linalg.cholesky(top_full)]
    pallas_call x0 -> x2, Pallas kernels: none -> 69 us  [the longest x1 54.6 us: per_device(): pl.pallas_call(lambda *refs: chol_kernel(n_col, *refs), out_shape=(jax.Sh...]
    another operation x44 -> x0, matrix products: 62 us -> none  [the longest x30 38.9 us: solve_right(): return jax.scipy.linalg.solve_triangular(factor, values.T, lower=True).T]
    all_gather x2 -> x1, waiting for transfers between devices: 92 us -> 65.5 us  [per_device(): lax.all_gather(top_part, ('row', 'layer', 'col'), axis=0, tiled=False)]
    another operation x33 -> x0, local copies, waits for them, and re-layouts: 25.6 us -> none
    all_gather x1, waiting for transfers between devices: 0.02 us -> 20.5 us  [per_device(): rest_full = lax.all_gather(rest_part, 'col', axis=1, tiled=True)]
    psum x1, waiting for transfers between devices: 57.8 us -> 46.6 us  [per_device(): win_sum = lax.psum(panel_win[0], 'layer')]
    all_to_all x1 -> x0, waiting for transfers between devices: 8.62 us -> none  [per_device(): lax.all_to_all(factor_rest, 'layer', split_axis=1, concat_axis=0, tiled=T...]
  transfers between devices with their start and end apart: 8 -> 7, of which waited for: 6 -> 5; matrix products, arithmetic and copies ran while one was open for 57% -> 0% of each run, Pallas kernels for 0% -> 19%
where the time goes in v1:
time: 293 us
  waiting for transfers between devices  197 us (67%)
  Pallas kernels  69 us (24%)
  between operations  14.2 us (5%)
  local copies, waits for them, and re-layouts  12.5 us (4%)
    all_gather x1, waiting for transfers between devices, per_device(): lax.all_gather(top_part, ('row', 'layer', 'col'), axis=0, tiled=False)  65.5 us
    pallas_call x1, Pallas kernels, per_device(): pl.pallas_call(lambda *refs: chol_kernel(n_col, *refs), out_shape=(jax.Sh...  54.6 us
    psum x1, waiting for transfers between devices, per_device(): win_sum = lax.psum(panel_win[0], 'layer')  46.6 us
    reduce_scatter x1, waiting for transfers between devices, per_device(): lax.psum_scatter(panel_rest[0], 'layer', scatter_dimension=0, tiled=True)  32.2 us
    reduce_scatter x1, waiting for transfers between devices, per_device(): lax.psum_scatter(panel_top[0], 'layer', scatter_dimension=0, tiled=True)  30.4 us
    all_gather x1, waiting for transfers between devices, per_device(): rest_full = lax.all_gather(rest_part, 'col', axis=1, tiled=True)  20.5 us
    pallas_call x1, Pallas kernels, per_device(): pl.pallas_call(solve_kernel, out_shape=(jax.ShapeDtypeStruct(window.shape...  14.4 us
    unnamed x13, local copies, waits for them, and re-layouts  10.9 us
  transfers between devices with their start and end apart: 7, of which 5 were waited for; matrix products, arithmetic and copies ran while one was open for 0% of the time, Pallas kernels for 19%

profile of v1, /device:TPU:0, one launch (start us, length us, event | category | flops | bytes accessed | tf_op | source)
XLA Modules:
  0.0 292.8 jit_solution(1370896870333748840)
XLA Ops:
  7.2 0.0 reduce-scatter.4.cloned.1.call-start
  7.2 0.7 reduce-scatter.4.cloned.1.call-update
  7.9 0.0 all-gather.9.cloned.1.call-start
  7.9 30.4 %reduce-scatter.4.cloned.1.call-done = f32[128,256]{1,0:T(8,128)} async-done(((f32[512,256]{1,0:T(8,128)}), f32[128,256]{1,0:T(8,128)}) %reduce-scatter.4.cloned.1.call-update) | async-done | bytes 131088 | tf_op jit(solution)/shard_map/reduce_scatter | solution.py:105
  38.4 0.0 all-gather.9.cloned.1.call-update
  38.4 0.0 all-reduce.2.cloned.1.call-start
  38.4 65.5 %all-gather.9.cloned.1.call-done = f32[4096,256]{1,0:T(8,128)} async-done(((f32[128,256]{1,0:T(8,128)}), f32[4096,256]{1,0:T(8,128)}) %all-gather.9.cloned.1.call-update) | async-done | bytes 4194320 | tf_op jit(solution)/shard_map/all_gather | solution.py:106
  103.9 0.0 all-reduce.2.cloned.1.call-update
  103.9 0.0 reduce-scatter.6.cloned.1.call-start
  104.0 0.5 reduce-scatter.6.cloned.1.call-update
  104.5 0.0 all-gather.5.cloned.1.call-start
  104.6 46.6 %all-reduce.2.cloned.1.call-done = f32[256,512]{1,0:T(8,128)} async-done(((f32[256,512]{1,0:T(8,128)}), f32[256,512]{1,0:T(8,128)}) %all-reduce.2.cloned.1.call-update) | async-done | bytes 524304 | tf_op jit(solution)/shard_map/psum | solution.py:112
  151.1 0.0 all-gather.5.cloned.1.call-update
  151.1 0.0 reduce-scatter.8.cloned.1.call-start
  151.2 0.5 reduce-scatter.8.cloned.1.call-update
  151.7 0.0 all-gather.7.cloned.1.call-start
  151.8 32.2 %reduce-scatter.6.cloned.1.call-done = f32[336,256]{1,0:T(8,128)} async-done(((f32[1344,256]{1,0:T(8,128)}), f32[336,256]{1,0:T(8,128)}) %reduce-scatter.6.cloned.1.call-update) | async-done | bytes 344080 | tf_op jit(solution)/shard_map/reduce_scatter | solution.py:110
  183.9 0.0 all-gather.7.cloned.1.call-update
  183.9 0.0 copy-start.5
  184.0 2.2 copy-done.5
  186.1 54.6 %factor.1 = (f32[1024,1024]{1,0:T(8,128)S(1)}, f32[8,128,128]{2,1,0:T(8,128)S(1)}) custom-call(f32[32,128,256]{2,1,0:T(8,128)S(1)} %bitcast.7), custom_call_target="tpu_custom_call" | custom-call | flops 85899345920 | bytes 12582912 | tf_op jit(solution)/shard_map/factor/pallas_call | solution.py:117
  240.8 0.0 copy-start
  240.8 2.0 copy-done
  242.8 1.0 copy.8
  243.8 0.0 all-gather.5.cloned.1.call-done.win_ref
  243.8 0.0 reduce-scatter.8.cloned.1.call-done.trail_ref
  243.8 20.5 %all-gather.7.cloned.1.call-done.rest_ref = f32[336,1024]{1,0:T(8,128)} async-done(((f32[336,256]{1,0:T(8,128)}), f32[336,1024]{1,0:T(8,128)}) %all-gather.7.cloned.1.call-update) | async-done | bytes 1376272 | tf_op jit(solution)/shard_map/all_gather | solution.py:111
  264.2 0.0 copy-start.1
  264.2 2.2 copy-done.1
  266.4 0.0 copy-start.2
  266.4 1.3 copy-done.2
  267.8 0.0 copy-start.3
  267.8 1.2 copy-done.3
  269.0 0.0 copy-start.4
  269.0 1.0 copy-done.4
  270.0 14.4 %solve.1 = (f32[256,1024]{1,0:T(8,128)S(1)}, f32[336,1024]{1,0:T(8,128)S(1)}, f32[336,256]{1,0:T(8,128)}) custom-call(f32[256,1024]{1,0:T(8,128)S(1)} %copy-done.3, f32[336,1024]{1,0:T(8,128)S(1)} %copy-done.2, f32[336,256]{1,0:T(8,128)S(1)} %copy-done.4, f32[1024,1024]{1,0:T(8,128)S(1)} %copy-done.1, f32[8,128,128]{2,1,0:T(8,128)S(1)} %get-tuple-element.18.inv_ref), custom_call_target="tpu_custom_call" | custom-call | tf_op jit(solution)/shard_map/solve/pallas_call | solution.py:132
  284.4 0.8 constant_dynamic-slice_fusion.1
  285.2 0.8 constant_dynamic-slice_fusion
  (1 shorter events, 0.0 us)
Async XLA Ops:
  7.2 31.2 %reduce-scatter.4.cloned.1.call-start = ((), (), s32[]{:S(2)}) async-start(), calls=%async_computation.3 | async-start | bytes 655360 | tf_op jit(solution)/shard_map/reduce_scatter | solution.py:105
  7.9 96.0 %all-gather.9.cloned.1.call-start = ((), (), s32[]{:S(2)}) async-start(), calls=%async_computation.9 | async-start | bytes 4325376 | tf_op jit(solution)/shard_map/all_gather | solution.py:106
  38.4 112.7 %all-reduce.2.cloned.1.call-start = ((), (), s32[]{:S(2)}) async-start(), calls=%async_computation.4 | async-start | bytes 1048576 | tf_op jit(solution)/shard_map/psum | solution.py:112
  103.9 80.0 %reduce-scatter.6.cloned.1.call-start = ((), (), s32[]{:S(2)}) async-start(), calls=%async_computation.6 | async-start | bytes 1720320 | tf_op jit(solution)/shard_map/reduce_scatter | solution.py:110
  104.5 139.3 %all-gather.5.cloned.1.call-start = ((), (), s32[]{:S(2)}) async-start(), calls=%async_computation.5 | async-start | bytes 1572864 | tf_op jit(solution)/shard_map/all_gather | solution.py:113
  151.1 92.6 %reduce-scatter.8.cloned.1.call-start = ((), (), s32[]{:S(2)}) async-start(), calls=%async_computation.8 | async-start | bytes 1720320 | tf_op jit(solution)/shard_map/reduce_scatter | solution.py:114
  151.7 112.5 %all-gather.7.cloned.1.call-start = ((), (), s32[]{:S(2)}) async-start(), calls=%async_computation.7 | async-start | bytes 1720320 | tf_op jit(solution)/shard_map/all_gather | solution.py:111
  183.9 2.2 copy-start.5
  240.8 2.0 copy-start
  264.2 2.2 copy-start.1
  266.4 1.3 copy-start.2
  267.8 1.2 copy-start.3
  269.0 1.0 copy-start.4
Sparse Core Ops, SparseCore 0:
  10.8 27.4 reduce-scatter.3
  41.8 62.0 all-gather.8
  107.2 43.8 all-reduce.1
  154.2 29.7 reduce-scatter.5
  185.4 9.0 all-gather.4
  197.5 31.1 reduce-scatter.7
  230.3 33.9 all-gather.6
